TPU v7x, 32 devices: a whole 2x2x4 slice. The times are simulated.
32 devices in a mesh: sec: 4 (over y, core), dp: 4 (over z), mp: 2 (over x).
Axes of the slice: x: 2, y: 2, z: 4, core: 2. Of those that a mesh axis runs over, the one named last changes fastest.
Arguments:
- policy_query: bfloat16 [16, 128, 4096], P(('sec', 'dp'), None, 'mp'), may hold values from -6 to 6
- policy_memory: bfloat16 [2, 16, 128, 1024], P(None, ('sec', 'dp'), None, 'mp'), may hold values from -6 to 6
- chosen_output_rows: bfloat16 [16, 128, 4096], P(('sec', 'dp'), None, 'mp'), may hold values from -0.09375 to 0.09375
- adapter_rows: bfloat16 [16, 128, 8192], P(('sec', 'dp'), None, 'mp'), may hold values from -6 to 6
- adapter_down: bfloat16 [4096, 64], P('mp'), may hold values from -0.09375 to 0.09375
- adapter_up: bfloat16 [64, 8192], P(None, 'mp'), may hold values from -0.0078125 to 0.0078125
- scorer_query: bfloat16 [4, 4, 4, 128, 4096], P('sec', None, 'dp', None, 'mp'), may hold values from -6 to 6
- scorer_key_values: bfloat16 [4, 2, 4, 4, 128, 1024], P('sec', None, None, 'dp', None, 'mp'), may hold values from -6 to 6
- score_heads: float32 [2, 4096], P(None, 'mp'), may hold values from -0.1875 to 0.1875
- document_ids: int32 [4, 4, 128], P(None, 'dp'), may hold values from 0 to 3, never falling along the last dimension, each value on 1 to 64 neighbouring positions
- prompt_lengths: int32 [4, 4, 4], P(None, 'dp'), may hold values from 1 to 31
Outputs:
- advantages: float32 [16, 128], P(('sec', 'dp'))
- query_grad: bfloat16 [16, 128, 4096], P(('sec', 'dp'), None, 'mp')
- memory_grad: bfloat16 [2, 16, 128, 1024], P(None, ('sec', 'dp'), None, 'mp')
- down_grad: float32 [4096, 64], P('mp')
- up_grad: float32 [64, 8192], P(None, 'mp')
Inputs may be any that keep to these rules, and one draw needn't show every extreme that they name: `document_ids`: within each row the document numbers never fall; every document has 1 to 64 positions and one has exactly 64.
All inputs are finite; a program needn't handle non-finite values.
Results may differ from a plain program's by a relative error of at most 0.0081.
Values may be sent and summed in bfloat16 or wider, within the bound.
A program may use at most 64 MiB of HBM per device.

v0:
```python
import jax
import jax.numpy as jnp
from jax import lax
from jax.sharding import PartitionSpec as P

HEAD_DIM = 128


kl_weight = 0.1
trace_decay = 0.95
epsilon = 1e-05
masked_score = -1e30


def span_masks(document_index, prompt):
    length = document_index.shape[-1]
    labels = jnp.arange(prompt.shape[-1], dtype=jnp.int32)
    member = (document_index[:, None] == labels[None, :]).astype(jnp.float32)
    counts = jnp.sum(member, axis=0)
    firsts = jnp.cumsum(counts) - counts
    position = jnp.arange(length).astype(jnp.float32)
    start_pos = jnp.sum(member * firsts[None, :], axis=1)
    prompt_pos = jnp.sum(member * prompt.astype(jnp.float32)[None, :], axis=1)
    ending = jnp.sum(member * (firsts + counts - 1.0)[None, :], axis=1)
    respond = (position - start_pos >= prompt_pos).astype(jnp.float32)
    closing = (position == ending).astype(jnp.float32)
    return (respond, closing)


def trace_matrix(document_index):
    length = document_index.shape[-1]
    position = jnp.arange(length, dtype=jnp.int32)
    later = position[None, :] - position[:, None]
    linked = (document_index[:, None] == document_index[None, :]) & (later >= 0)
    powers = jnp.power(jnp.float32(trace_decay), jnp.maximum(later, 0).astype(jnp.float32))
    return jnp.where(linked, powers, jnp.float32(0.0))


def attend_section(query, keys, values, document_index):
    length = query.shape[0]
    kv_heads = keys.shape[1] // HEAD_DIM
    groups = query.shape[1] // keys.shape[1]
    query_h = query.reshape(length, kv_heads, groups, HEAD_DIM)
    keys_h = keys.reshape(length, kv_heads, HEAD_DIM)
    values_h = values.reshape(length, kv_heads, HEAD_DIM)
    scores = jnp.einsum(
        "qcgd,kcd->cgqk", query_h, keys_h, preferred_element_type=jnp.float32
    ) * HEAD_DIM ** (-0.5)
    position = jnp.arange(length, dtype=jnp.int32)
    allowed = (document_index[:, None] == document_index[None, :]) & (
        position[:, None] >= position[None, :]
    )
    scores = jnp.where(allowed, scores, masked_score)
    top = jnp.max(scores, axis=-1, keepdims=True)
    raised = jnp.exp(scores - top)
    probs = raised / jnp.sum(raised, axis=-1, keepdims=True)
    probs_b = probs.astype(jnp.bfloat16)
    attended = jnp.einsum(
        "cgqk,kcd->qcgd", probs_b, values_h, preferred_element_type=jnp.float32
    ).reshape(length, -1)
    return (attended, probs, probs_b)


def attend_back(query, keys, values, probs, probs_b, grad_b):
    length = query.shape[0]
    kv_heads = keys.shape[1] // HEAD_DIM
    groups = query.shape[1] // keys.shape[1]
    query_h = query.reshape(length, kv_heads, groups, HEAD_DIM)
    keys_h = keys.reshape(length, kv_heads, HEAD_DIM)
    values_h = values.reshape(length, kv_heads, HEAD_DIM)
    grad_h = grad_b.reshape(length, kv_heads, groups, HEAD_DIM)
    dprobs = jnp.einsum("qcgd,kcd->cgqk", grad_h, values_h, preferred_element_type=jnp.float32)
    inner = jnp.sum(probs * dprobs, axis=-1, keepdims=True)
    dscores = (probs * (dprobs - inner)).astype(jnp.bfloat16)
    scale = HEAD_DIM ** (-0.5)
    query_grad = (
        (jnp.einsum("cgqk,kcd->qcgd", dscores, keys_h, preferred_element_type=jnp.float32) * scale)
        .astype(jnp.bfloat16)
        .reshape(length, -1)
    )
    keys_grad = (
        (jnp.einsum("cgqk,qcgd->kcd", dscores, query_h, preferred_element_type=jnp.float32) * scale)
        .astype(jnp.bfloat16)
        .reshape(length, -1)
    )
    values_grad = (
        jnp.einsum("cgqk,qcgd->kcd", probs_b, grad_h, preferred_element_type=jnp.float32)
        .astype(jnp.bfloat16)
        .reshape(length, -1)
    )
    return (query_grad, keys_grad, values_grad)


def on_device(
    policy_query,
    policy_memory,
    chosen_output_rows,
    adapter_rows,
    adapter_down,
    adapter_up,
    scorer_query,
    scorer_key_values,
    score_heads,
    document_ids,
    prompt_lengths,
):
    highest = lax.Precision.HIGHEST
    section_index = lax.axis_index("sec")
    docs_all = document_ids[:, 0, :]
    prompts_all = prompt_lengths[:, 0, :]
    own_doc = lax.dynamic_index_in_dim(docs_all, section_index, 0, keepdims=False)
    own_prompt = lax.dynamic_index_in_dim(prompts_all, section_index, 0, keepdims=False)
    query = policy_query[0]
    keys = policy_memory[0, 0]
    values = policy_memory[1, 0]
    chosen_float = chosen_output_rows[0].astype(jnp.float32)
    down_float = adapter_down.astype(jnp.float32)
    rows_all = lax.all_gather(chosen_output_rows, "sec", axis=0, tiled=True)
    head_pick = lax.dynamic_index_in_dim(
        score_heads, jnp.maximum(section_index - 2, 0), 0, keepdims=False
    )

    def score_row_values(item_list):
        scorer_query_rows, scorer_keys, scorer_values, document_index, chosen_token = item_list
        scorer_attended, scorer_probs, scorer_probs_batch = attend_section(
            scorer_query_rows, scorer_keys, scorer_values, document_index
        )
        by_rows = jnp.sum(scorer_attended * chosen_token.astype(jnp.float32), axis=1)
        by_head = jnp.dot(scorer_attended, head_pick, precision=highest)
        return jnp.where(section_index < 2, by_rows, by_head)

    partials = lax.map(
        score_row_values,
        (
            scorer_query[0, :, 0],
            scorer_key_values[0, 0, :, 0],
            scorer_key_values[0, 1, :, 0],
            docs_all,
            rows_all,
        ),
    )
    attended, probs, probs_b = attend_section(query, keys, values, own_doc)
    base_part = jnp.sum(attended * chosen_float, axis=1)
    in_part = jnp.dot(attended, down_float, precision=highest)
    out_part = jnp.einsum(
        "ld,rd->lr", adapter_rows[0], adapter_up, preferred_element_type=jnp.float32
    )
    summed = lax.psum(partials, "mp")
    scores = lax.all_to_all(summed, "sec", split_axis=0, concat_axis=0, tiled=True)
    base, lowrank_in, lowrank_out = lax.psum((base_part, in_part, out_part), "mp")
    policy_new = base + jnp.sum(lowrank_in * lowrank_out, axis=-1)
    policy_old = scores[0]
    policy_ref = scores[1]
    reward = scores[2]
    value = scores[3]
    respond, closing = span_masks(own_doc, own_prompt)
    next_value = jnp.concatenate([value[1:], jnp.zeros((1,), jnp.float32)]) * (1.0 - closing)
    delta = -kl_weight * (policy_old - policy_ref) + closing * reward + next_value - value
    advantage = jnp.dot(trace_matrix(own_doc), delta, precision=highest)
    count, total, square_total = lax.psum(
        (jnp.sum(respond), jnp.sum(respond * advantage), jnp.sum(respond * advantage * advantage)),
        ("sec", "dp"),
    )
    mean = total / count
    spread = square_total / count - mean * mean
    whitened = respond * (advantage - mean) * lax.rsqrt(spread + epsilon)
    ratio = jnp.exp(policy_new - policy_old)
    grad_score = -respond * ratio * whitened / count
    scaled_out = grad_score[:, None] * lowrank_out
    down_part = jnp.einsum("lh,lr->hr", attended, scaled_out, precision=highest)
    scaled_in = (grad_score[:, None] * lowrank_in).astype(jnp.bfloat16)
    up_part = jnp.einsum(
        "lr,ld->rd", scaled_in, adapter_rows[0], preferred_element_type=jnp.float32
    )
    down_grad, up_grad = lax.psum((down_part, up_part), ("sec", "dp"))
    grad_attended = (
        grad_score[:, None] * chosen_float + jnp.dot(scaled_out, down_float.T, precision=highest)
    ).astype(jnp.bfloat16)
    query_grad, keys_grad, values_grad = attend_back(
        query, keys, values, probs, probs_b, grad_attended
    )
    memory_grad = jnp.stack([keys_grad, values_grad])[:, None]
    return (whitened[None, :], query_grad[None], memory_grad, down_grad, up_grad)


def solution(mesh):
    return jax.shard_map(
        on_device,
        mesh=mesh,
        in_specs=(
            P(("sec", "dp"), None, "mp"),
            P(None, ("sec", "dp"), None, "mp"),
            P(("sec", "dp"), None, "mp"),
            P(("sec", "dp"), None, "mp"),
            P("mp", None),
            P(None, "mp"),
            P("sec", None, "dp", None, "mp"),
            P("sec", None, None, "dp", None, "mp"),
            P(None, "mp"),
            P(None, "dp", None),
            P(None, "dp", None),
        ),
        out_specs=(
            P(("sec", "dp"), None),
            P(("sec", "dp"), None, "mp"),
            P(None, ("sec", "dp"), None, "mp"),
            P("mp", None),
            P(None, "mp"),
        ),
        check_vma=False,
    )
```

profile of v0, /device:TPU:0, one launch (start us, length us, event | category | flops | bytes accessed | tf_op | source)
XLA Modules:
  0.0 258.1 jit_solution(17690354571835321051)
XLA Ops:
  8.0 2.2 copy.93
  10.2 2.4 fusion.73
  12.6 2.1 copy.125
  14.6 2.0 copy.126
  16.7 2.5 copy.86
  20.1 1.4 copy.128
  24.9 2.1 fusion.75
  27.0 2.8 %fusion.28 = (f32[128]{0:T(128)}, f32[4,4,128,128]{2,3,1,0:T(8,128)S(1)}) fusion(f32[128,4,4,128]{0,3,2,1:T(8,128)} %bitcast.267, bf16[128,4,128,1]{0,2,3,1:T(8,128)(2,1)} %bitcast.277, f32[4,4,128]{2,1,0:T(4,128)} %get-tuple-element.195, bf16[128,4,128,1]{0,2,3,1:T(8,128)(2,1)S(1)} %bitcast.269, bf16[128,4,4,128]{0,3,2,1:T(8,128)(2,1)S(1)} %bitcast.263, ...), kind=kOutput, calls=%fused_computation.47 | convolution fusion | flops 136054784 | bytes 2908672 | tf_op jit(solution)/shard_map/cgqk,kcd->qcgd/dot_general | solution.py:58
  32.0 2.9 %all-gather.2.cloned.1.call-done = bf16[4,128,2048]{2,1,0:T(8,128)(2,1)} async-done(((bf16[1,128,2048]{2,1,0:T(8,128)(2,1)}), bf16[4,128,2048]{2,1,0:T(8,128)(2,1)}) %all-gather.2.cloned.1.call-update) | async-done | bytes 2097168 | tf_op jit(solution)/shard_map/all_gather | solution.py:118
  34.9 44.1 %while.12 = (s32[]{:T(128)}, f32[4,128]{1,0:T(4,128)}, pred[]{:T(512)}, bf16[4,128,512]{1,2,0:T(8,128)(2,1)}, s32[4,128]{1,0:T(4,128)}, /*index=5*/bf16[4,128,51...) while((s32[]{:T(128)}, f32[4,128]{1,0:T(4,128)}, ...), condition=%wide.region_8.9_spmd, body=%wide.region_4.8_spmd.sunk | while | flops 207669504 | bytes 9941158 | solution.py:132
  40.6 2.1 fusion.130
  42.8 1.9 fusion.131
  51.6 2.1 fusion.130
  53.8 1.9 fusion.131
  55.7 1.3 dynamic_update_slice.7
  62.7 2.1 fusion.130
  64.8 1.9 fusion.131
  66.7 1.3 dynamic_update_slice.7
  73.7 2.1 fusion.130
  75.8 1.9 fusion.131
  79.9 19.6 %all-reduce.8.cloned.1.call-done = (f32[4,1,128]{2,1,0:T(1,128)}, f32[128]{0:T(128)}, f32[128,64]{0,1:T(8,128)}, f32[128,64]{0,1:T(8,128)}) async-done(((f32[4,1,128]{2,1,0:T(1,128)}, f32[128]{0:T(128)}, f32[128,64]{0,1:T(8,128)}, f32[128,64]{0,1:T(8,128)}), (f32[4,1,128]{2,1,0:T(1,128)}, f32[128]{0:T(128)}, f32[128,64]{0,1:T(8,128)}, f32[128,64]{0,1:T(8,128)})) %all-reduce.8.cloned.1.call-update) | async-done | bytes 68112 | tf_op jit(solution)/shard_map/psum | solution.py:148
  99.5 3.4 %all-to-all-start = ((f32[4,1,128]{2,1,0:T(1,128)}), f32[4,1,128]{2,1,0:T(1,128)S(1)}, u32[]{:S(2)}, u32[]{:S(2)}) async-start(f32[4,1,128]{2,1,0:T(1,128)} %get-tuple-element.178), calls=%async_computation | async-start | bytes 4096 | tf_op jit(solution)/shard_map/all_to_all | solution.py:149
  103.7 2.9 %all-to-all-done = f32[4,1,128]{2,1,0:T(1,128)S(1)} async-done(((f32[4,1,128]{2,1,0:T(1,128)}), f32[4,1,128]{2,1,0:T(1,128)S(1)}, u32[]{:S(2)}, u32[]{:S(2)}) %all-to-all-start) | async-done | bytes 2080 | tf_op jit(solution)/shard_map/all_to_all | solution.py:149
  106.7 1.6 select_reduce_fusion.3
  108.3 32.4 %all-reduce = (f32[]{:T(128)}, f32[]{:T(128)}, f32[]{:T(128)}) all-reduce(f32[]{:T(128)} %get-tuple-element.150, f32[]{:T(128)} %get-tuple-element.151, f32[]{:T(128)} %get-tuple-element.149), channel_id=1, replica_groups=mesh['sec'=4,'dp'=4,'mp'=2] {'sec','dp'}, use_global_device_ids=true, to_apply=%region_16.17 | all-reduce | flops 3 | bytes 24 | tf_op jit(solution)/shard_map/psum | solution.py:160
  143.3 1.8 multiply_divide_fusion
  145.1 1.8 fusion.15
  146.9 2.9 %fusion.42 = f32[2048,64]{0,1:T(8,128)} fusion(f32[128,2048]{0,1:T(8,128)S(1)} %bitcast.260, f32[128,64]{0,1:T(8,128)} %get-tuple-element.181, f32[128]{0:T(128)S(1)} %get-tuple-element.191), kind=kOutput, calls=%fused_computation.71 | convolution fusion | flops 201334784 | bytes 1606144 | tf_op jit(solution)/shard_map/lh,lr->hr/dot_general | solution.py:170
  154.1 1.4 fusion.23
  156.9 90.6 %all-reduce.6.cloned.1.call-done = (f32[2048,64]{0,1:T(8,128)}, f32[64,4096]{1,0:T(8,128)}) async-done(((f32[2048,64]{0,1:T(8,128)}, f32[64,4096]{1,0:T(8,128)}), (f32[2048,64]{0,1:T(8,128)}, f32[64,4096]{1,0:T(8,128)})) %all-reduce.6.cloned.1.call-update) | async-done | bytes 1572880 | tf_op jit(solution)/shard_map/psum | solution.py:175
  247.4 1.9 copy.145
  249.3 2.3 copy.146
  (109 shorter events, 39.9 us)
Async XLA Ops:
  7.2 23.7 %copy-start = (bf16[1,128,4096]{2,1,0:T(8,128)(2,1)S(1)}, bf16[1,128,4096]{2,1,0:T(8,128)(2,1)}, u32[]{:S(2)}) copy-start(bf16[1,128,4096]{2,1,0:T(8,128)(2,1)} %param.16) | copy-start | bytes 3145732
  7.2 27.7 %all-gather.2.cloned.1.call-start = ((), (), s32[]{:S(2)}) async-start(), calls=%async_computation.1 | async-start | bytes 2621440 | tf_op jit(solution)/shard_map/all_gather | solution.py:118
  7.9 91.6 %all-reduce.8.cloned.1.call-start = ((), (), s32[]{:S(2)}) async-start(), calls=%async_computation.3 | async-start | bytes 136192 | tf_op jit(solution)/shard_map/psum | solution.py:148
  10.2 6.5 %copy-start.3 = (bf16[1,4,1,128,2048]{4,3,2,1,0:T(8,128)(2,1)S(1)}, bf16[1,4,1,128,2048]{4,3,2,1,0:T(8,128)(2,1)}, u32[]{:S(2)}) copy-start(bf16[1,4,1,128,2048]{4,3,2,1,0:T(8,128)(2,1)} %param.19) | copy-start | bytes 6291460
  16.7 2.5 copy-start.11
  19.2 5.0 %copy-start.17 = (f32[2,2048]{1,0:T(2,128)S(1)}, f32[2,2048]{1,0:T(2,128)}, u32[]{:S(2)}) copy-start(f32[2,2048]{1,0:T(2,128)} %param.21) | copy-start | bytes 49156
  21.4 8.3 %copy-start.4 = (bf16[1,128,2048]{1,2,0:T(8,128)(2,1)}, bf16[1,128,2048]{1,2,0:T(8,128)(2,1)S(1)}, u32[]{:S(2)}) copy-start(bf16[1,128,2048]{1,2,0:T(8,128)(2,1)S(1)} %copy.128) | copy-start | bytes 1572868
  22.1 4.8 %copy-start.16 = (s32[128]{0:T(128)}, s32[128]{0:T(128)S(1)}, u32[]{:S(2)}) copy-start(s32[128]{0:T(128)S(1)} %fusion.49) | copy-start | bytes 1540
  24.9 4.9 %copy-start.14 = (pred[128,128]{0,1:T(8,128)(4,1)}, pred[128,128]{0,1:T(8,128)(4,1)S(1)}, u32[]{:S(2)}) copy-start(pred[128,128]{0,1:T(8,128)(4,1)S(1)} %compare_and_fusion) | copy-start | bytes 49156
  27.0 2.8 %copy-start.8 = (bf16[2048,64]{0,1:T(8,128)(2,1)S(1)}, bf16[2048,64]{0,1:T(8,128)(2,1)}, u32[]{:S(2)}) copy-start(bf16[2048,64]{0,1:T(8,128)(2,1)} %param.17) | copy-start | bytes 786436
  27.0 3.9 %copy-start.9 = (bf16[64,4096]{1,0:T(8,128)(2,1)S(1)}, bf16[64,4096]{1,0:T(8,128)(2,1)}, u32[]{:S(2)}) copy-start(bf16[64,4096]{1,0:T(8,128)(2,1)} %param.18) | copy-start | bytes 1572868
  29.7 5.2 %copy-start.1 = (f32[4,4,128,128]{2,3,1,0:T(8,128)}, f32[4,4,128,128]{2,3,1,0:T(8,128)S(1)}, u32[]{:S(2)}) copy-start(f32[4,4,128,128]{2,3,1,0:T(8,128)S(1)} %get-tuple-element.198) | copy-start | bytes 3145732
  40.6 2.2 copy-start.10
  51.6 2.2 copy-start.10
  62.6 2.2 copy-start.10
  73.7 2.2 copy-start.10
  79.0 67.9 %copy-start.2 = (f32[4,4,128,128]{2,3,1,0:T(8,128)S(1)}, f32[4,4,128,128]{2,3,1,0:T(8,128)}, u32[]{:S(2)}) copy-start(f32[4,4,128,128]{2,3,1,0:T(8,128)} %copy-done.1) | copy-start | bytes 3145732
  99.5 50.3 %copy-start.12 = (f32[128,64]{0,1:T(8,128)S(1)}, f32[128,64]{0,1:T(8,128)}, u32[]{:S(2)}) copy-start(f32[128,64]{0,1:T(8,128)} %get-tuple-element.180) | copy-start | bytes 98308
  99.5 7.1 %all-to-all-start = ((f32[4,1,128]{2,1,0:T(1,128)}), f32[4,1,128]{2,1,0:T(1,128)S(1)}, u32[]{:S(2)}, u32[]{:S(2)}) async-start(f32[4,1,128]{2,1,0:T(1,128)} %get-tuple-element.178), calls=%async_computation | async-start | bytes 4096 | tf_op jit(solution)/shard_map/all_to_all | solution.py:149
  102.9 144.5 %all-reduce.6.cloned.1.call-start = ((), (), s32[]{:S(2)}) async-start(), calls=%async_computation.2 | async-start | bytes 3145728 | tf_op jit(solution)/shard_map/psum | solution.py:175
  146.9 4.4 %copy-start.13 = (bf16[1,1,128,512]{2,3,1,0:T(8,128)(2,1)S(1)}, bf16[1,1,128,512]{2,3,1,0:T(8,128)(2,1)}, u32[]{:S(2)}) copy-start(bf16[1,1,128,512]{2,3,1,0:T(8,128)(2,1)} %copy.91) | copy-start | bytes 393220
  146.9 4.4 %copy-start.15 = (f32[4,4,128]{2,1,0:T(4,128)S(1)}, f32[4,4,128]{2,1,0:T(4,128)}, u32[]{:S(2)}) copy-start(f32[4,4,128]{2,1,0:T(4,128)} %get-tuple-element.195) | copy-start | bytes 24580
  149.8 1.6 copy-start.6
  151.4 1.2 copy-start.7
  152.8 1.3 copy-start.5
Sparse Core Ops, SparseCore 0:
  9.6 25.2 all-gather.1
  79.1 20.3 all-reduce.7
  153.0 94.4 all-reduce.5
where the time goes:
time: 260 us; the launch traced here: 258 us
  waiting for transfers between devices  117 us (45%)
  local copies, waits for them, and re-layouts  43 us (17%)
  matrix products  38.9 us (15%)
  blocking collectives  32.4 us (12%)
  between operations  16.6 us (6%)
  other arithmetic  6.77 us (3%)
  starting transfers between devices  3.48 us (1%)
    psum x1, waiting for transfers between devices, on_device(): down_grad, up_grad = lax.psum((down_part, up_part), ('sec', 'dp'))  90.6 us
    psum x1, blocking collectives, on_device(): lax.psum((jnp.sum(respond), jnp.sum(respond * advantage), jnp.sum(respond...  32.4 us
    psum x1, waiting for transfers between devices, on_device(): summed = lax.psum(partials, 'mp')  19.6 us
    dynamic_slice x16, local copies, waits for them, and re-layouts, on_device(): lax.map(score_row_values, (scorer_query[0, :, 0], scorer_key_values[0, 0,...  13.7 us
    unnamed x41, local copies, waits for them, and re-layouts  12.8 us
    dot_general x5, matrix products, attend_section(): jnp.einsum('cgqk,kcd->qcgd', probs_b, values_h, preferred_element_type=jn...  11.4 us
    dot_general x4, matrix products, score_row_values(): by_head = jnp.dot(scorer_attended, head_pick, precision=highest)  7.48 us
    sub x5, matrix products, attend_section(): raised = jnp.exp(scores - top)  6.58 us
  transfers between devices with their start and end apart: 4, of which 4 were waited for; matrix products, arithmetic and copies ran while one was open for 11% of the time, Pallas kernels for 0%

commit v1 on v0

v1 whole, which is shorter than its diff:
```python
import functools
import math

import jax
import jax.numpy as jnp
from jax import lax
from jax.experimental import pallas as pl
from jax.experimental.pallas import tpu as pltpu
from jax.sharding import PartitionSpec as P

HEAD_DIM = 128
kl_weight = 0.1
trace_decay = 0.95
epsilon = 1e-05
masked_score = -1e30
F32, BF16 = jnp.float32, jnp.bfloat16
MESH = pl.DeviceIdType.MESH


def nn(a, b):
    return jnp.dot(a, b, preferred_element_type=F32)


def nt(a, b):
    return lax.dot_general(a, b, (((1,), (1,)), ((), ())), preferred_element_type=F32)


def tn(a, b):
    return lax.dot_general(a, b, (((0,), (0,)), ((), ())), preferred_element_type=F32)


def split(a):
    high = a.astype(BF16)
    return high, (a - high.astype(F32)).astype(BF16)


def kernel(S, N, M, L,
           q_ref, kv_ref, chosen_ref, rows_ref, down_ref, up_ref, sq_ref, skv_ref, heads_ref, docs_ref, prompts_ref,
           adv_ref, qg_ref, mg_ref, dg_ref, ug_ref,
           att, patt, probs, chosen_rx, score_tx, score_rx, pack_tx, pack_rx, mom_rx,
           both, tx1, rx1, tx2, rx2, txz, rxz, fin, grad,
           c_send, c_recv, s_send, s_recv, p_send, p_recv, m_send, m_recv, h_send, h_recv, z_send, z_recv, g_send,
           g_recv, a_send, a_recv):
    T = q_ref.shape[0]
    HQ = q_ref.shape[1]
    KV = kv_ref.shape[2]
    heads = KV // HEAD_DIM
    groups = HQ // KV
    RANK = down_ref.shape[1]
    DOCS = prompts_ref.shape[2]
    sec, dp, mp = lax.axis_index("sec"), lax.axis_index("dp"), lax.axis_index("mp")
    scale = HEAD_DIM ** (-0.5)

    def add(x, d, n):
        return lax.rem(x + d, n) if d else x

    offsets = [(s, d, 0) for s in range(S) for d in range(N) if s or d]
    offsets += [(s, 0, m) for s in range(S) for m in range(1, M)]
    barrier = pltpu.get_barrier_semaphore()
    for s, d, m in offsets:
        pl.semaphore_signal(barrier, inc=1, device_id=(add(sec, s, S), add(dp, d, N), add(mp, m, M)),
                            device_id_type=MESH)
    pl.semaphore_wait(barrier, len(offsets))

    half = S // 2
    pair = 1 - lax.rem(sec, 2)

    def chosen_copy(src, slot, k, target):
        return pltpu.make_async_remote_copy(src, chosen_rx.at[slot], c_send.at[k], c_recv.at[k],
                                            device_id=(target, dp, mp), device_id_type=MESH)

    @pl.when(sec >= half)
    def _():
        chosen_copy(chosen_ref, sec, 0, lax.rem(sec, half)).start()

    @pl.when(sec < half)
    def _():
        chosen_copy(chosen_ref, sec, 1, pair).start()
        chosen_rx[sec] = chosen_ref[...]

    q_pos = lax.broadcasted_iota(jnp.int32, (T, T), 0)
    k_pos = lax.broadcasted_iota(jnp.int32, (T, T), 1)

    def docs_of(j):
        row = jnp.broadcast_to(docs_ref[j].astype(F32), (T, T))
        return row, row.T

    def attend(q, k, v, allowed):
        scores = jnp.where(allowed, nt(q, k) * scale, masked_score)
        raised = jnp.exp(scores - jnp.max(scores, axis=-1, keepdims=True))
        p = raised * (1.0 / jnp.sum(raised, axis=-1, keepdims=True))
        return p, nn(p.astype(BF16), v)

    def stack(ref, c):
        return jnp.concatenate(
            [ref[:, (c * groups + g) * HEAD_DIM:(c * groups + g + 1) * HEAD_DIM] for g in range(groups)], axis=0)

    def score_row(j, carry):
        row, col = docs_of(j)
        allowed = jnp.concatenate([(row == col) & (q_pos >= k_pos)] * groups, axis=0)
        for c in range(heads):
            cs = slice(c * HEAD_DIM, (c + 1) * HEAD_DIM)
            _, out = attend(stack(sq_ref.at[j], c), skv_ref[0, j, :, cs], skv_ref[1, j, :, cs], allowed)
            att[j, c] = out
        return carry

    lax.fori_loop(0, S, score_row, 0)

    @pl.when(sec < half)
    def _():
        chosen_copy(chosen_ref, sec, 0, pair).wait_recv()
        chosen_copy(chosen_rx.at[sec + half], sec + half, 2, pair).start()

    row, col = docs_of(sec)
    allowed = jnp.concatenate([(row == col) & (q_pos >= k_pos)] * groups, axis=0)
    base_acc = jnp.zeros((T, HEAD_DIM), F32)
    low_in = jnp.zeros((T, RANK), F32)
    for c in range(heads):
        cs = slice(c * HEAD_DIM, (c + 1) * HEAD_DIM)
        p, out = attend(stack(q_ref, c), kv_ref[0, :, cs], kv_ref[1, :, cs], allowed)
        probs[c] = p
        for g in range(groups):
            hs = slice((c * groups + g) * HEAD_DIM, (c * groups + g + 1) * HEAD_DIM)
            part = out[g * T:(g + 1) * T]
            patt[:, hs] = part
            base_acc += part * chosen_ref[:, hs].astype(F32)
    high, low = split(patt[...])
    low_in = nn(high, down_ref[...]) + nn(low, down_ref[...])
    low_out = nt(rows_ref[...], up_ref[...])
    pack_tx[...] = jnp.concatenate([low_in, low_out], axis=1)

    def pack_copy(m):
        return pltpu.make_async_remote_copy(pack_tx, pack_rx.at[m], p_send.at[m], p_recv.at[m],
                                            device_id=(sec, dp, add(mp, m, M)), device_id_type=MESH)

    for m in range(1, M):
        pack_copy(m).start()

    columns = jnp.where(k_pos == S, jnp.sum(base_acc, axis=1, keepdims=True), 0.0)
    grad[...] = columns

    @pl.when(sec < half)
    def _():
        chosen_copy(chosen_ref, sec, 1, pair).wait_recv()
        chosen_copy(chosen_ref, sec, 2, pair).wait_recv()
        for j in range(S):
            acc = jnp.zeros((T, HEAD_DIM), F32)
            for c in range(heads):
                for g in range(groups):
                    h = c * groups + g
                    acc += att[j, c, g * T:(g + 1) * T, :] * chosen_rx[
                        j, :, h * HEAD_DIM:(h + 1) * HEAD_DIM].astype(F32)
            grad[...] += jnp.where(k_pos == j, jnp.sum(acc, axis=1, keepdims=True), 0.0)

    @pl.when(sec >= half)
    def _():
        for j in range(S):
            acc = jnp.zeros((T, HEAD_DIM), F32)
            for c in range(heads):
                for g in range(groups):
                    h = c * groups + g
                    both_heads = heads_ref[:, h * HEAD_DIM:(h + 1) * HEAD_DIM]
                    acc += att[j, c, g * T:(g + 1) * T, :] * jnp.where(
                        sec == half, both_heads[0:1], both_heads[1:2])
            grad[...] += jnp.where(k_pos == j, jnp.sum(acc, axis=1, keepdims=True), 0.0)

    turned = grad[...].T
    sub = lax.broadcasted_iota(jnp.int32, (8, T), 0)
    for j in range(S):
        score_tx[j] = jnp.where(sub == 0, turned[j:j + 1, :], turned[S:S + 1, :])

    def score_copy(s, m):
        target = add(sec, s, S)
        return pltpu.make_async_remote_copy(score_tx.at[target], score_rx.at[s * M + m], s_send.at[s * M + m],
                                            s_recv.at[s * M + m],
                                            device_id=(target, dp, add(mp, m, M)), device_id_type=MESH)

    score_rx[0] = score_tx[sec]
    pairs = [(s, m) for s in range(S) for m in range(M) if s or m]
    for s, m in pairs:
        score_copy(s, m).start()

    lane = lax.broadcasted_iota(jnp.int32, (1, T), 1)
    doc = docs_ref[sec]
    start_pos = jnp.sum((col < row).astype(F32), axis=0, keepdims=True)
    ending = jnp.sum((col <= row).astype(F32), axis=0, keepdims=True) - 1.0
    prompt_row = prompts_ref[sec]
    prompt_pos = jnp.zeros((1, T), F32)
    for d in range(DOCS):
        prompt_pos += jnp.where(doc == d, prompt_row[:, d:d + 1].astype(F32), 0.0)
    position = lane.astype(F32)
    respond = (position - start_pos >= prompt_pos).astype(F32)
    closing = (position == ending).astype(F32)
    later = q_pos - k_pos
    trace = jnp.where((row == col) & (later >= 0),
                      jnp.exp(jnp.maximum(later, 0).astype(F32) * math.log(trace_decay)), 0.0)

    for m in range(1, M):
        pack_copy(m).wait()
    packed = pack_tx[...]
    for m in range(1, M):
        packed = packed + pack_rx[m]
    low_in, low_out = packed[:, :RANK], packed[:, RANK:]
    low_sum = jnp.broadcast_to(jnp.sum(low_in * low_out, axis=1, keepdims=True), (T, T)).T[0:1, :]

    for s, m in pairs:
        score_copy(s, m).wait()

    def section(k):
        slot = lax.rem(sec - k + S, S) * M
        total = score_rx[slot]
        for m in range(1, M):
            total = total + score_rx[slot + m]
        return total[0:1, :]

    base = score_rx[0]
    for m in range(1, M):
        base = base + score_rx[m]
    policy_new = base[1:2, :] + low_sum
    old, ref, reward, value = section(0), section(1), section(2), section(3)
    value8 = jnp.broadcast_to(value, (8, T))
    next_value = jnp.where(lane == T - 1, 0.0, pltpu.roll(value8, T - 1, 1)[0:1, :]) * (1.0 - closing)
    delta = -kl_weight * (old - ref) + closing * reward + next_value - value
    advantage = jnp.sum(trace * jnp.broadcast_to(delta, (T, T)).T, axis=0, keepdims=True)
    count = jnp.sum(respond, axis=1, keepdims=True)
    total = jnp.sum(respond * advantage, axis=1, keepdims=True)
    square = jnp.sum(respond * advantage * advantage, axis=1, keepdims=True)
    mom_rx[0] = jnp.where(sub == 0, count, jnp.where(sub == 1, total, square))

    def mom_copy(s, d):
        k = s * N + d
        return pltpu.make_async_remote_copy(mom_rx.at[0], mom_rx.at[k], m_send.at[k], m_recv.at[k],
                                            device_id=(add(sec, s, S), add(dp, d, N), mp), device_id_type=MESH)

    peers = [(s, d) for s in range(S) for d in range(N) if s or d]
    for s, d in peers:
        mom_copy(s, d).start()
    for s, d in peers:
        mom_copy(s, d).wait()
    moments = jnp.sum(mom_rx[...], axis=0)
    count, total, square = moments[0:1], moments[1:2], moments[2:3]
    mean = total / count
    spread = square / count - mean * mean
    whitened = respond * (advantage - mean) * lax.rsqrt(spread + epsilon)
    adv_ref[...] = whitened
    grad_score = -respond * jnp.exp(policy_new - old) * whitened / count
    gs = jnp.broadcast_to(grad_score, (T, T)).T

    scaled_out = gs[:, :RANK] * low_out
    scaled_in = gs[:, :RANK] * low_in
    turned = jnp.concatenate([scaled_out, scaled_in], axis=1).T
    out_high, out_low = split(turned[:RANK])
    in_t = turned[RANK:].astype(BF16)
    D = rows_ref.shape[1]
    for p in range(S * N):
        lo, hi = p * L, (p + 1) * L
        a, b = min(lo, HQ), min(hi, HQ)
        if b > a:
            high, low = split(patt[:, a:b])
            both[p, :, a - lo:b - lo] = nn(out_high, high) + nn(out_low, high) + nn(out_high, low)
        a, b = max(lo, HQ), min(hi, HQ + D)
        if b > a:
            both[p, :, a - lo:b - lo] = nn(in_t, rows_ref[:, a - HQ:b - HQ])
        a = max(lo, HQ + D)
        if hi > a:
            both[p, :, a - lo:] = jnp.zeros((RANK, hi - a), F32)

    b0, b1 = lax.rem(sec, 2), sec // 2
    near, far = sec + 1 - 2 * b0, lax.rem(sec + half, S)
    Q, H = N, 2 * N

    def block_copy(src, dst, k, target):
        return pltpu.make_async_remote_copy(src, dst, h_send.at[k], h_recv.at[k],
                                            device_id=(target, dp, mp), device_id_type=MESH)

    tx1[...] = both[pl.ds((1 - b0) * H, H)].astype(BF16)
    copy1 = block_copy(tx1, rx1, 0, near)
    copy1.start()

    so_high, so_low = split(scaled_out)

    def back(c):
        cs = slice(c * HEAD_DIM, (c + 1) * HEAD_DIM)
        down_c = down_ref[c * groups * HEAD_DIM:(c + 1) * groups * HEAD_DIM, :]
        through = nt(so_high, down_c) + nt(so_low, down_c)
        g = jnp.concatenate(
            [gs * chosen_ref[:, (c * groups + i) * HEAD_DIM:(c * groups + i + 1) * HEAD_DIM].astype(F32)
             + through[:, i * HEAD_DIM:(i + 1) * HEAD_DIM] for i in range(groups)], axis=0).astype(BF16)
        p = probs[c]
        k, v = kv_ref[0, :, cs], kv_ref[1, :, cs]
        dprobs = nt(g, v)
        inner = jnp.sum(p * dprobs, axis=-1, keepdims=True)
        ds = (p * (dprobs - inner)).astype(BF16)
        qg = (nn(ds, k) * scale).astype(BF16)
        for i in range(groups):
            qg_ref[:, (c * groups + i) * HEAD_DIM:(c * groups + i + 1) * HEAD_DIM] = qg[i * T:(i + 1) * T]
        mg_ref[0, :, cs] = (tn(ds, stack(q_ref, c)) * scale).astype(BF16)
        mg_ref[1, :, cs] = tn(p.astype(BF16), g).astype(BF16)

    todo = list(range(heads))

    def some(n):
        for _ in range(min(n, len(todo))):
            back(todo.pop(0))

    some(1)
    copy1.wait()
    mine = b0 * H
    tx2[...] = (both[pl.ds(mine + (1 - b1) * Q, Q)] + rx1[pl.ds((1 - b1) * Q, Q)].astype(F32)).astype(BF16)
    copy2 = block_copy(tx2, rx2, 1, far)
    copy2.start()
    mine = mine + b1 * Q
    both[pl.ds(mine, Q)] += rx1[pl.ds(b1 * Q, Q)].astype(F32)
    some(2)
    copy2.wait()
    both[pl.ds(mine, Q)] += rx2[...].astype(F32)
    txz[...] = both[pl.ds(mine, Q)].astype(BF16)

    def z_copy(d):
        target = add(dp, d, N)
        return pltpu.make_async_remote_copy(txz.at[target], rxz.at[d], z_send.at[d], z_recv.at[d],
                                            device_id=(sec, target, mp), device_id_type=MESH)

    for d in range(1, N):
        z_copy(d).start()
    some(heads)
    for d in range(1, N):
        z_copy(d).wait()
    own = both[mine + dp]
    for d in range(1, N):
        own = own + rxz[d].astype(F32)
    fin[mine + dp] = own.astype(BF16)

    def g_copy(d):
        return pltpu.make_async_remote_copy(fin.at[mine + dp], fin.at[mine + dp], g_send.at[d], g_recv.at[d],
                                            device_id=(sec, add(dp, d, N), mp), device_id_type=MESH)

    for d in range(1, N):
        g_copy(d).start()
    for d in range(1, N):
        g_copy(d).wait()

    def a_copy(k, start, size, target):
        ref = fin.at[pl.ds(start, size)]
        return pltpu.make_async_remote_copy(ref, ref, a_send.at[k], a_recv.at[k],
                                            device_id=(target, dp, mp), device_id_type=MESH)

    copy3 = a_copy(0, mine, Q, far)
    copy3.start()
    copy3.wait()
    copy4 = a_copy(1, b0 * H, H, near)
    copy4.start()
    copy4.wait()
    for p in range(S * N):
        lo, hi = p * L, (p + 1) * L
        a, b = min(lo, HQ), min(hi, HQ)
        if b > a:
            dg_ref[:, a:b] = fin[p, :, a - lo:b - lo].astype(F32)
        a, b = max(lo, HQ), min(hi, HQ + D)
        if b > a:
            ug_ref[:, a - HQ:b - HQ] = fin[p, :, a - lo:b - lo].astype(F32)

    @pl.when(sec >= half)
    def _():
        chosen_copy(chosen_ref, sec, 0, lax.rem(sec, half)).wait_send()

    @pl.when(sec < half)
    def _():
        chosen_copy(chosen_ref, sec, 1, pair).wait_send()
        chosen_copy(chosen_rx.at[sec + half], sec + half, 2, pair).wait_send()


def on_device(S, N, M, query, memory, chosen, rows, down, up, squery, skv, score_heads, docs, prompts):
    T, HQ = query.shape[1:]
    KV = memory.shape[3]
    D, RANK = rows.shape[2], down.shape[1]
    heads, groups = KV // HEAD_DIM, HQ // KV
    pieces = S * N
    L = -(-(HQ + D) // (pieces * 128)) * 128
    dma = pltpu.SemaphoreType.DMA
    vm = pltpu.VMEM
    outs = pl.pallas_call(
        functools.partial(kernel, S, N, M, L),
        out_shape=(
            jax.ShapeDtypeStruct((1, T), F32),
            jax.ShapeDtypeStruct((T, HQ), BF16),
            jax.ShapeDtypeStruct((2, T, KV), BF16),
            jax.ShapeDtypeStruct((RANK, HQ), F32),
            jax.ShapeDtypeStruct((RANK, D), F32),
        ),
        in_specs=[pl.BlockSpec(memory_space=pltpu.VMEM)] * 11,
        out_specs=[pl.BlockSpec(memory_space=pltpu.VMEM)] * 5,
        scratch_shapes=[
            vm((S, heads, groups * T, HEAD_DIM), F32), vm((T, HQ), F32), vm((heads, groups * T, T), F32),
            vm((S, T, HQ), BF16), vm((S, 8, T), F32), vm((S * M, 8, T), F32), vm((T, 2 * RANK), F32),
            vm((M, T, 2 * RANK), F32), vm((pieces, 8, T), F32),
            vm((pieces, RANK, L), F32), vm((pieces // 2, RANK, L), BF16), vm((pieces // 2, RANK, L), BF16),
            vm((N, RANK, L), BF16), vm((N, RANK, L), BF16), vm((N, RANK, L), BF16), vm((N, RANK, L), BF16),
            vm((pieces, RANK, L), BF16), vm((T, T), F32),
            dma((3,)), dma((3,)), dma((S * M,)), dma((S * M,)), dma((M,)), dma((M,)), dma((pieces,)), dma((pieces,)),
            dma((2,)), dma((2,)), dma((N,)), dma((N,)), dma((N,)), dma((N,)), dma((2,)), dma((2,)),
        ],
        compiler_params=pltpu.CompilerParams(collective_id=0, has_side_effects=True,
                                             vmem_limit_bytes=56 * 1024 * 1024),
    )(query[0], memory[:, 0], chosen[0], rows[0], down, up, squery[0, :, 0], skv[0, :, :, 0], score_heads,
      docs, prompts)
    adv, qg, mg, dg, ug = outs
    return adv, qg[None], mg[:, None], dg.T, ug


def solution(mesh):
    S, N, M = (mesh.shape[a] for a in ("sec", "dp", "mp"))
    return jax.shard_map(
        functools.partial(on_device, S, N, M),
        mesh=mesh,
        in_specs=(
            P(("sec", "dp"), None, "mp"),
            P(None, ("sec", "dp"), None, "mp"),
            P(("sec", "dp"), None, "mp"),
            P(("sec", "dp"), None, "mp"),
            P("mp", None),
            P(None, "mp"),
            P("sec", None, "dp", None, "mp"),
            P("sec", None, None, "dp", None, "mp"),
            P(None, "mp"),
            P(None, "dp", None),
            P(None, "dp", None),
        ),
        out_specs=(
            P(("sec", "dp"), None),
            P(("sec", "dp"), None, "mp"),
            P(None, ("sec", "dp"), None, "mp"),
            P("mp", None),
            P(None, "mp"),
        ),
        check_vma=False,
    )
```

time: 260 us -> 71 us (0.27)
  waiting for transfers between devices: 117 us -> 0 us
  Pallas kernels: 0 us -> 60.4 us
  matrix products: 38.9 us -> 0 us
  local copies, waits for them, and re-layouts: 43 us -> 9.62 us
  blocking collectives: 32.4 us -> 0 us
  between operations: 16.6 us -> 0.65 us
  other arithmetic: 6.77 us -> 0 us
  starting transfers between devices: 3.48 us -> 0 us
    psum x2 -> x0, waiting for transfers between devices: 110 us -> none  [the longest x1 90.6 us: on_device(): down_grad, up_grad = lax.psum((down_part, up_part), ('sec', 'dp'))]
    pallas_call x0 -> x1, Pallas kernels: none -> 60.4 us  [on_device(): pl.pallas_call(functools.partial(kernel, S, N, M, L), out_shape=(jax.Shap...]
    psum x1 -> x0, blocking collectives: 32.4 us -> none  [on_device(): lax.psum((jnp.sum(respond), jnp.sum(respond * advantage), jnp.sum(respond...]
    dot_general x23 -> x0, matrix products: 32.3 us -> none  [the longest x5 11.4 us: attend_section(): jnp.einsum('cgqk,kcd->qcgd', probs_b, values_h, preferred_element_type=jn...]
    dynamic_slice x17 -> x0, local copies, waits for them, and re-layouts: 14.3 us -> none  [the longest x16 13.7 us: on_device(): lax.map(score_row_values, (scorer_query[0, :, 0], scorer_key_values[0, 0,...]
    sub x5 -> x0, matrix products: 6.58 us -> none  [attend_section(): raised = jnp.exp(scores - top)]
    dynamic_update_slice x4 -> x0, local copies, waits for them, and re-layouts: 5.17 us -> none  [on_device(): lax.map(score_row_values, (scorer_query[0, :, 0], scorer_key_values[0, 0,...]
    eq x5 -> x0, local copies, waits for them, and re-layouts: 3.46 us -> none  [the longest x4 2.77 us: attend_section(): document_index[:, None] == document_index[None, :]]
  transfers between devices with their start and end apart: 4 -> 0, of which waited for: 4 -> 0; matrix products, arithmetic and copies ran while one was open for 11% -> 0% of each run, Pallas kernels for 0% -> 0%
where the time goes in v1:
time: 71 us; the launch traced here: 70.7 us
  Pallas kernels  60.4 us (85%)
  local copies, waits for them, and re-layouts  9.62 us (14%)
    pallas_call x1, Pallas kernels, on_device(): pl.pallas_call(functools.partial(kernel, S, N, M, L), out_shape=(jax.Shap...  60.4 us
    unnamed x8, local copies, waits for them, and re-layouts  9.62 us

profile of v1, /device:TPU:0, one launch (start us, length us, event | category | flops | bytes accessed | tf_op | source)
XLA Modules:
  0.0 70.7 jit_solution(8906241638083613667)
XLA Ops:
  0.6 2.0 %copy.16.down_ref = bf16[2048,64]{1,0:T(8,128)(2,1)} copy(bf16[2048,64]{0,1:T(8,128)(2,1)} %param.15) | data formatting | bytes 524288 | tf_op args[4]
  2.6 60.4 %shard_map.146 = (f32[1,128]{1,0:T(1,128)}, bf16[128,2048]{1,0:T(8,128)(2,1)}, bf16[2,128,512]{2,1,0:T(8,128)(2,1)}, f32[64,2048]{1,0:T(8,128)}, f32[64,4096]{1,0:T(8,128)}) custom-call(bf16[128,2048]{1,0:T(8,128)(2,1)} %bitcast.16, bf16[2,128,512]{2,1,0:T(8,128)(2,1)} %bitcast.18, bf16[128,2048]{1,0:T(8,128)(2,1)} %bitcast.17, bf16[128,4096]{1,0:T(8,128)(2,1)} %bitcast.12, ...), custom_call_target="tpu_custom_call" | custom-call | tf_op jit(solution)/shard_map/pallas_call | solution.py:382
  63.0 0.0 copy-start
  63.0 1.3 %copy.23 = f32[1,128]{1,0:T(1,128)} copy(f32[1,128]{1,0:T(1,128)} %get-tuple-element.25) | data formatting | bytes 1024
  64.3 1.9 %copy.24 = bf16[1,128,2048]{2,1,0:T(8,128)(2,1)} copy(bf16[1,128,2048]{2,1,0:T(8,128)(2,1)} %bitcast.15) | data formatting | bytes 1048576
  66.2 1.7 %copy.25 = bf16[2,1,128,512]{3,2,1,0:T(8,128)(2,1)} copy(bf16[2,1,128,512]{3,2,1,0:T(8,128)(2,1)} %bitcast.19) | data formatting | bytes 524288
  67.9 1.9 %copy.26 = f32[2048,64]{0,1:T(8,128)} copy(f32[2048,64]{0,1:T(8,128)} %bitcast.14) | data formatting | bytes 1048576
  69.7 0.0 copy-done
  69.7 1.0 %copy.27 = f32[64,4096]{1,0:T(8,128)} copy(f32[64,4096]{1,0:T(8,128)S(1)} %copy-done) | data formatting | bytes 2097152
Async XLA Ops:
  63.0 6.7 %copy-start = (f32[64,4096]{1,0:T(8,128)S(1)}, f32[64,4096]{1,0:T(8,128)}, u32[]{:S(2)}) copy-start(f32[64,4096]{1,0:T(8,128)} %get-tuple-element.29) | copy-start | bytes 3145732

commit v2 on v1

--- a/solution.py
+++ b/solution.py
@@ -36,17 +36,17 @@
 
 def kernel(S, N, M, L,
            q_ref, kv_ref, chosen_ref, rows_ref, down_ref, up_ref, sq_ref, skv_ref, heads_ref, docs_ref, prompts_ref,
-           adv_ref, qg_ref, mg_ref, dg_ref, ug_ref,
+           adv_ref, qg_ref, mg_ref, sum_ref,
            att, patt, probs, chosen_rx, score_tx, score_rx, pack_tx, pack_rx, mom_rx,
            both, tx1, rx1, tx2, rx2, txz, rxz, fin, grad,
-           c_send, c_recv, s_send, s_recv, p_send, p_recv, m_send, m_recv, h_send, h_recv, z_send, z_recv, g_send,
+           c_send, c_recv, s_send, s_recv, p_send, p_recv, m_send, m_recv, h_send, h_recv, f_send, f_recv, z_send, z_recv, g_send,
            g_recv, a_send, a_recv):
     T = q_ref.shape[0]
     HQ = q_ref.shape[1]
     KV = kv_ref.shape[2]
     heads = KV // HEAD_DIM
     groups = HQ // KV
-    RANK = down_ref.shape[1]
+    RANK = down_ref.shape[0]
     DOCS = prompts_ref.shape[2]
     sec, dp, mp = lax.axis_index("sec"), lax.axis_index("dp"), lax.axis_index("mp")
     scale = HEAD_DIM ** (-0.5)
@@ -125,7 +125,7 @@
             patt[:, hs] = part
             base_acc += part * chosen_ref[:, hs].astype(F32)
     high, low = split(patt[...])
-    low_in = nn(high, down_ref[...]) + nn(low, down_ref[...])
+    low_in = nt(high, down_ref[...]) + nt(low, down_ref[...])
     low_out = nt(rows_ref[...], up_ref[...])
     pack_tx[...] = jnp.concatenate([low_in, low_out], axis=1)
 
@@ -267,7 +267,7 @@
 
     b0, b1 = lax.rem(sec, 2), sec // 2
     near, far = sec + 1 - 2 * b0, lax.rem(sec + half, S)
-    Q, H = N, 2 * N
+    Q, H = N, half * N
 
     def block_copy(src, dst, k, target):
         return pltpu.make_async_remote_copy(src, dst, h_send.at[k], h_recv.at[k],
@@ -281,8 +281,8 @@
 
     def back(c):
         cs = slice(c * HEAD_DIM, (c + 1) * HEAD_DIM)
-        down_c = down_ref[c * groups * HEAD_DIM:(c + 1) * groups * HEAD_DIM, :]
-        through = nt(so_high, down_c) + nt(so_low, down_c)
+        down_c = down_ref[:, c * groups * HEAD_DIM:(c + 1) * groups * HEAD_DIM]
+        through = nn(so_high, down_c) + nn(so_low, down_c)
         g = jnp.concatenate(
             [gs * chosen_ref[:, (c * groups + i) * HEAD_DIM:(c * groups + i + 1) * HEAD_DIM].astype(F32)
              + through[:, i * HEAD_DIM:(i + 1) * HEAD_DIM] for i in range(groups)], axis=0).astype(BF16)
@@ -307,27 +307,35 @@
     copy1.wait()
     mine = b0 * H
     tx2[...] = (both[pl.ds(mine + (1 - b1) * Q, Q)] + rx1[pl.ds((1 - b1) * Q, Q)].astype(F32)).astype(BF16)
-    copy2 = block_copy(tx2, rx2, 1, far)
-    copy2.start()
+    def far_copy(d):
+        t = add(dp, d, N)
+        return pltpu.make_async_remote_copy(tx2.at[t], rx2.at[t], f_send.at[d], f_recv.at[d],
+                                            device_id=(far, dp, mp), device_id_type=MESH)
+
+    order = list(range(1, N)) + [0]
+    for d in order:
+        far_copy(d).start()
     mine = mine + b1 * Q
     both[pl.ds(mine, Q)] += rx1[pl.ds(b1 * Q, Q)].astype(F32)
-    some(2)
-    copy2.wait()
-    both[pl.ds(mine, Q)] += rx2[...].astype(F32)
-    txz[...] = both[pl.ds(mine, Q)].astype(BF16)
+    some(1)
 
     def z_copy(d):
         target = add(dp, d, N)
         return pltpu.make_async_remote_copy(txz.at[target], rxz.at[d], z_send.at[d], z_recv.at[d],
                                             device_id=(sec, target, mp), device_id_type=MESH)
 
-    for d in range(1, N):
-        z_copy(d).start()
+    for d in order:
+        far_copy(d).wait()
+        t = add(dp, d, N)
+        part = both[mine + t] + rx2[t].astype(F32)
+        if d:
+            txz[t] = part.astype(BF16)
+            z_copy(d).start()
+        else:
+            own = part
     some(heads)
     for d in range(1, N):
         z_copy(d).wait()
-    own = both[mine + dp]
-    for d in range(1, N):
         own = own + rxz[d].astype(F32)
     fin[mine + dp] = own.astype(BF16)
 
@@ -335,39 +343,69 @@
         return pltpu.make_async_remote_copy(fin.at[mine + dp], fin.at[mine + dp], g_send.at[d], g_recv.at[d],
                                             device_id=(sec, add(dp, d, N), mp), device_id_type=MESH)
 
+    def a_copy(k, piece, target):
+        return pltpu.make_async_remote_copy(fin.at[piece], fin.at[piece], a_send.at[k], a_recv.at[k],
+                                            device_id=(target, dp, mp), device_id_type=MESH)
+
+    other = b0 * H + (1 - b1) * Q
+    sent = []
+
+    def go(copy):
+        copy.start()
+        sent.append(copy)
+
     for d in range(1, N):
         g_copy(d).start()
-    for d in range(1, N):
-        g_copy(d).wait()
-
-    def a_copy(k, start, size, target):
-        ref = fin.at[pl.ds(start, size)]
-        return pltpu.make_async_remote_copy(ref, ref, a_send.at[k], a_recv.at[k],
-                                            device_id=(target, dp, mp), device_id_type=MESH)
-
-    copy3 = a_copy(0, mine, Q, far)
-    copy3.start()
-    copy3.wait()
-    copy4 = a_copy(1, b0 * H, H, near)
-    copy4.start()
-    copy4.wait()
+    for d in range(N):
+        source = lax.rem(dp - d + N, N) if d else dp
+        if d:
+            g_copy(d).wait()
+        go(a_copy(d, mine + source, far))
+        go(a_copy(N + d, mine + source, near))
+    for d in range(N):
+        source = lax.rem(dp - d + N, N) if d else dp
+        a_copy(d, mine + source, far).wait_recv()
+        go(a_copy(2 * N + d, other + source, near))
+    for d in range(N):
+        a_copy(N + d, mine, near).wait_recv()
+        a_copy(2 * N + d, mine, near).wait_recv()
+    for copy in sent:
+        copy.wait_send()
+    sum_ref[...] = fin[...]
+
+    @pl.when(sec >= half)
+    def _():
+        chosen_copy(chosen_ref, sec, 0, lax.rem(sec, half)).wait_send()
+
+    @pl.when(sec < half)
+    def _():
+        chosen_copy(chosen_ref, sec, 1, pair).wait_send()
+        chosen_copy(chosen_rx.at[sec + half], sec + half, 2, pair).wait_send()
+
+
+def finish(S, N, L, adv_in, qg_in, mg_in, sum_in, adv_ref, qg_ref, mg_ref, dg_ref, ug_ref):
+    adv_ref[...] = adv_in[...]
+    qg_ref[...] = qg_in[...]
+    mg_ref[...] = mg_in[...]
+    HQ, D = dg_ref.shape[1], ug_ref.shape[1]
     for p in range(S * N):
         lo, hi = p * L, (p + 1) * L
         a, b = min(lo, HQ), min(hi, HQ)
         if b > a:
-            dg_ref[:, a:b] = fin[p, :, a - lo:b - lo].astype(F32)
+            dg_ref[:, a:b] = sum_in[p, :, a - lo:b - lo].astype(F32)
         a, b = max(lo, HQ), min(hi, HQ + D)
         if b > a:
-            ug_ref[:, a - HQ:b - HQ] = fin[p, :, a - lo:b - lo].astype(F32)
-
-    @pl.when(sec >= half)
-    def _():
-        chosen_copy(chosen_ref, sec, 0, lax.rem(sec, half)).wait_send()
-
-    @pl.when(sec < half)
-    def _():
-        chosen_copy(chosen_ref, sec, 1, pair).wait_send()
-        chosen_copy(chosen_rx.at[sec + half], sec + half, 2, pair).wait_send()
+            ug_ref[:, a - HQ:b - HQ] = sum_in[p, :, a - lo:b - lo].astype(F32)
+
+
+def outs_shape(T, HQ, KV, RANK, D):
+    return (
+        jax.ShapeDtypeStruct((1, T), F32),
+        jax.ShapeDtypeStruct((T, HQ), BF16),
+        jax.ShapeDtypeStruct((2, T, KV), BF16),
+        jax.ShapeDtypeStruct((RANK, HQ), F32),
+        jax.ShapeDtypeStruct((RANK, D), F32),
+    )
 
 
 def on_device(S, N, M, query, memory, chosen, rows, down, up, squery, skv, score_heads, docs, prompts):
@@ -385,11 +423,10 @@
             jax.ShapeDtypeStruct((1, T), F32),
             jax.ShapeDtypeStruct((T, HQ), BF16),
             jax.ShapeDtypeStruct((2, T, KV), BF16),
-            jax.ShapeDtypeStruct((RANK, HQ), F32),
-            jax.ShapeDtypeStruct((RANK, D), F32),
+            jax.ShapeDtypeStruct((pieces, RANK, L), BF16),
         ),
         in_specs=[pl.BlockSpec(memory_space=pltpu.VMEM)] * 11,
-        out_specs=[pl.BlockSpec(memory_space=pltpu.VMEM)] * 5,
+        out_specs=[pl.BlockSpec(memory_space=pltpu.VMEM)] * 4,
         scratch_shapes=[
             vm((S, heads, groups * T, HEAD_DIM), F32), vm((T, HQ), F32), vm((heads, groups * T, T), F32),
             vm((S, T, HQ), BF16), vm((S, 8, T), F32), vm((S * M, 8, T), F32), vm((T, 2 * RANK), F32),
@@ -398,13 +435,21 @@
             vm((N, RANK, L), BF16), vm((N, RANK, L), BF16), vm((N, RANK, L), BF16), vm((N, RANK, L), BF16),
             vm((pieces, RANK, L), BF16), vm((T, T), F32),
             dma((3,)), dma((3,)), dma((S * M,)), dma((S * M,)), dma((M,)), dma((M,)), dma((pieces,)), dma((pieces,)),
-            dma((2,)), dma((2,)), dma((N,)), dma((N,)), dma((N,)), dma((N,)), dma((2,)), dma((2,)),
+            dma((1,)), dma((1,)), dma((N,)), dma((N,)), dma((N,)), dma((N,)), dma((N,)), dma((N,)),
+            dma((3 * N,)), dma((3 * N,)),
         ],
         compiler_params=pltpu.CompilerParams(collective_id=0, has_side_effects=True,
                                              vmem_limit_bytes=56 * 1024 * 1024),
-    )(query[0], memory[:, 0], chosen[0], rows[0], down, up, squery[0, :, 0], skv[0, :, :, 0], score_heads,
+    )(query[0], memory[:, 0], chosen[0], rows[0], down.T, up, squery[0, :, 0], skv[0, :, :, 0], score_heads,
       docs, prompts)
-    adv, qg, mg, dg, ug = outs
+    vmem = pl.BlockSpec(memory_space=pltpu.VMEM)
+    adv, qg, mg, dg, ug = pl.pallas_call(
+        functools.partial(finish, S, N, L),
+        out_shape=outs_shape(T, HQ, KV, RANK, D),
+        in_specs=[vmem] * 4,
+        out_specs=[vmem] * 5,
+        compiler_params=pltpu.CompilerParams(vmem_limit_bytes=32 * 1024 * 1024),
+    )(*outs)
     return adv, qg[None], mg[:, None], dg.T, ug
 
 

time: 71 us -> 62 us (0.87)
  local copies, waits for them, and re-layouts: 9.62 us -> 3.73 us
  Pallas kernels: 60.4 us -> 57.3 us
    unnamed x8, local copies, waits for them, and re-layouts: 9.62 us -> 3.73 us
    pallas_call x1, Pallas kernels: 60.4 us -> 55.8 us  [on_device(): pl.pallas_call(functools.partial(kernel, S, N, M, L), out_shape=(jax.Shap...]
    pallas_call x0 -> x1, Pallas kernels: none -> 1.53 us  [on_device(): pl.pallas_call(functools.partial(finish, S, N, L), out_shape=outs_shape(T...]
where the time goes in v2:
time: 62 us; the launch traced here: 61.7 us
  Pallas kernels  57.3 us (92%)
  local copies, waits for them, and re-layouts  3.73 us (6%)
  between operations  0.66 us (1%)
    pallas_call x1, Pallas kernels, on_device(): pl.pallas_call(functools.partial(kernel, S, N, M, L), out_shape=(jax.Shap...  55.8 us
    unnamed x8, local copies, waits for them, and re-layouts  3.73 us
    pallas_call x1, Pallas kernels, on_device(): pl.pallas_call(functools.partial(finish, S, N, L), out_shape=outs_shape(T...  1.53 us

profile of v2, /device:TPU:0, one launch (start us, length us, event | category | flops | bytes accessed | tf_op | source)
XLA Modules:
  0.0 61.7 jit_solution(14062854779851558232)
XLA Ops:
  0.6 55.8 %shard_map.146 = (f32[1,128]{1,0:T(1,128)}, bf16[128,2048]{1,0:T(8,128)(2,1)}, bf16[2,128,512]{2,1,0:T(8,128)(2,1)}, bf16[16,64,384]{2,1,0:T(8,128)(2,1)}) custom-call(bf16[128,2048]{1,0:T(8,128)(2,1)} %bitcast.15, bf16[2,128,512]{2,1,0:T(8,128)(2,1)} %bitcast.17, bf16[128,2048]{1,0:T(8,128)(2,1)} %bitcast.16, bf16[128,4096]{1,0:T(8,128)(2,1)} %bitcast.13, ...), custom_call_target="tpu_custom_call" | custom-call | tf_op jit(solution)/shard_map/pallas_call | solution.py:420
  56.4 0.0 copy-start
  56.4 1.1 %copy-done = bf16[16,64,384]{2,1,0:T(8,128)(2,1)S(1)} copy-done((bf16[16,64,384]{2,1,0:T(8,128)(2,1)S(1)}, bf16[16,64,384]{2,1,0:T(8,128)(2,1)}, u32[]{:S(2)}) %copy-start) | copy-done | bytes 786456
  57.6 0.0 copy-start.1
  57.6 1.0 %copy-done.1 = bf16[128,2048]{1,0:T(8,128)(2,1)S(1)} copy-done((bf16[128,2048]{1,0:T(8,128)(2,1)S(1)}, bf16[128,2048]{1,0:T(8,128)(2,1)}, u32[]{:S(2)}) %copy-start.1) | copy-done | bytes 524312
  58.6 0.0 copy-start.2
  58.6 0.9 %copy-done.2 = bf16[2,128,512]{2,1,0:T(8,128)(2,1)S(1)} copy-done((bf16[2,128,512]{2,1,0:T(8,128)(2,1)S(1)}, bf16[2,128,512]{2,1,0:T(8,128)(2,1)}, u32[]{:S(2)}) %copy-start.2) | copy-done | bytes 262168
  59.6 0.0 copy-start.3
  59.6 0.6 copy-done.3
  60.2 1.5 %shard_map.147 = (f32[1,128]{1,0:T(1,128)}, bf16[128,2048]{1,0:T(8,128)(2,1)}, bf16[2,128,512]{2,1,0:T(8,128)(2,1)}, f32[64,2048]{1,0:T(8,128)}, f32[64,4096]{1,0:T(8,128)}) custom-call(f32[1,128]{1,0:T(1,128)S(1)} %copy-done.3, bf16[128,2048]{1,0:T(8,128)(2,1)S(1)} %copy-done.1, bf16[2,128,512]{2,1,0:T(8,128)(2,1)S(1)} %copy-done.2, ...), custom_call_target="tpu_custom_call" | custom-call | tf_op jit(solution)/shard_map/pallas_call | solution.py:446
Async XLA Ops:
  56.4 1.1 %copy-start = (bf16[16,64,384]{2,1,0:T(8,128)(2,1)S(1)}, bf16[16,64,384]{2,1,0:T(8,128)(2,1)}, u32[]{:S(2)}) copy-start(bf16[16,64,384]{2,1,0:T(8,128)(2,1)} %get-tuple-element.17.sum_in) | copy-start | bytes 2359300
  57.6 1.0 %copy-start.1 = (bf16[128,2048]{1,0:T(8,128)(2,1)S(1)}, bf16[128,2048]{1,0:T(8,128)(2,1)}, u32[]{:S(2)}) copy-start(bf16[128,2048]{1,0:T(8,128)(2,1)} %get-tuple-element.15.qg_in) | copy-start | bytes 1572868
  58.6 0.9 %copy-start.2 = (bf16[2,128,512]{2,1,0:T(8,128)(2,1)S(1)}, bf16[2,128,512]{2,1,0:T(8,128)(2,1)}, u32[]{:S(2)}) copy-start(bf16[2,128,512]{2,1,0:T(8,128)(2,1)} %get-tuple-element.16.mg_in) | copy-start | bytes 786436
  59.6 0.6 %copy-start.3 = (f32[1,128]{1,0:T(1,128)S(1)}, f32[1,128]{1,0:T(1,128)}, u32[]{:S(2)}) copy-start(f32[1,128]{1,0:T(1,128)} %get-tuple-element.14.adv_in) | copy-start | bytes 1540
